TPU v7x, 32 devices: a whole 2x2x4 slice. The times are simulated.
32 devices in a mesh: vol: 2 (over y), space: 16 (over z, x, core).
Axes of the slice: x: 2, y: 2, z: 4, core: 2. Of those that a mesh axis runs over, the one named last changes fastest.
Arguments:
- volume: bfloat16 [2, 32, 64, 8, 128], P('vol', None, 'space'), may hold values from -80 to 80
- conv_weight: bfloat16 [32, 32, 3, 3, 3], replicated, may hold values from -0.21875 to 0.21875
- conv_bias: float32 [32], replicated, may hold values from -3 to 3
- basis: float32 [864, 864], replicated, may hold values from -3 to 3
- damping: float32 [1], replicated, may hold values from 0.5 to 2
Outputs:
- projected: float32 [864, 864], P('vol')
All inputs are finite; a program needn't handle non-finite values.
Results may differ from a plain program's by a relative error of at most 0.0019.
Values may be sent and summed in bfloat16 or wider, within the bound.
A program may use at most 64 MiB of HBM per device.

v0:
```python
import jax
import jax.numpy as jnp
from jax import lax
from jax.sharding import PartitionSpec as P


def shifted(block, axis, distance):
    devices = range(lax.axis_size(axis))
    route = [(i - distance, i) for i in devices if i - distance in devices]
    return lax.ppermute(block, axis, route)


def extract_patches(activated):
    chans, planes, rows_y, cols_z = activated.shape
    viewed = activated.reshape(chans, planes // 4, 4, rows_y // 4, 4, cols_z // 4, 4)[
        :, :, 1:, :, 1:, :, 1:
    ]
    viewed = viewed.transpose(0, 2, 4, 6, 1, 3, 5)
    return viewed.reshape(chans * 27, -1)


def body(volume, conv_weight, conv_bias, basis, damping):
    local_block = volume[0]
    from_above = shifted(local_block[:, 0:1], "space", -1)
    zero_plane = jnp.zeros_like(from_above)
    stacked = jnp.concatenate([zero_plane, local_block, from_above], axis=1)
    conv_out = lax.conv_general_dilated(
        stacked[None],
        conv_weight,
        (1, 1, 1),
        [(0, 0), (1, 1), (1, 1)],
        dimension_numbers=("NCDHW", "OIDHW", "NCDHW"),
        preferred_element_type=jnp.float32,
    )[0]
    activated = jnp.maximum(conv_out + conv_bias[:, None, None, None], 0.0).astype(jnp.bfloat16)
    patch_cols = extract_patches(activated)
    local_gram = jnp.dot(patch_cols, patch_cols.T, preferred_element_type=jnp.float32)
    gram_width = local_gram.shape[0]
    total_patches = patch_cols.shape[1] * lax.axis_size("space") * lax.axis_size("vol")
    panel_rows = gram_width // lax.axis_size("vol")
    row_start = lax.axis_index("vol") * panel_rows
    partial_rows = lax.psum_scatter(
        local_gram.astype(jnp.bfloat16), "vol", scatter_dimension=0, tiled=True
    ).astype(jnp.float32)
    row_panel = lax.psum(partial_rows, "space")
    diag_block = lax.dynamic_slice_in_dim(row_panel, row_start, panel_rows, 1)
    trace_value = lax.psum(jnp.trace(diag_block), "vol")
    normed_panel = row_panel / total_patches
    mean_diagonal = trace_value / total_patches / gram_width
    basis_rows = lax.dynamic_slice_in_dim(basis, row_start, panel_rows, 0)
    product = jnp.dot(
        normed_panel, basis, precision=lax.Precision.HIGHEST, preferred_element_type=jnp.float32
    )
    return product + damping[0] * mean_diagonal * basis_rows


def solution(mesh):
    in_specs = (P("vol", None, "space", None, None), P(), P(), P(), P())
    out_specs = P("vol", None)
    return jax.shard_map(body, mesh=mesh, in_specs=in_specs, out_specs=out_specs, check_vma=False)
```

profile of v0, /device:TPU:0, one launch (start us, length us, event | category | flops | bytes accessed | tf_op | source)
XLA Modules:
  0.0 149.4 jit_solution(2289497347999911215)
XLA Ops:
  6.5 0.0 copy-start
  6.5 0.0 reduce-scatter.2.cloned.1.call-start
  6.5 0.9 slice.10
  7.4 1.3 collective-permute-start
  8.7 1.8 %collective-permute-done = bf16[32,1,8,128]{3,2,1,0:T(8,128)(2,1)S(1)} collective-permute-done((bf16[32,1,8,128]{3,2,1,0:T(8,128)(2,1)S(1)}, bf16[32,1,8,128]{3,2,1,0:T(8,128)(2,1)S(1)}, u32[]{:S(2)}, u32[]{:S(2)}) %collective-permute-start) | collective-permute-done | bytes 65568 | tf_op jit(solution)/shard_map/ppermute | solution.py:10
  10.6 1.1 pad_maximum_fusion
  11.6 1.0 copy.21
  12.6 0.3 pad
  12.9 0.0 copy-start.2
  12.9 0.2 copy.23
  13.2 0.1 slice.11
  13.2 0.0 copy-done
  13.2 0.4 copy-done.2
  13.6 3.9 %fusion.10 = f32[4,8,8,17,32]{4,2,3,1,0:T(8,128)S(1)} fusion(bf16[32,32,3,3,3]{1,0,4,3,2:T(8,128)(2,1)S(1)} %copy-done, bf16[32,6,8,1,7,2]{0,4,5,2,1,3:T(8,128)(2,1)S(1)} %slice.11, bf16[32,6,8,1,8,17]{0,4,5,2,1,3:T(8,128)(2,1)S(1)} %copy.23, pred[8,17]{0,1:T(8,128)(4,1)S(1)} %copy-done.2), kind=kOutput, calls=%fused_computation.12 | convolution fusion | flops 222134272 | bytes 1073288 | tf_op jit(solution)/shard_map/conv_general_dilated | solution.py:27
  17.5 0.4 copy.24
  17.9 0.1 slice.12
  18.0 0.0 copy-start.1
  18.0 0.3 slice.13
  18.4 0.6 copy.30
  19.0 0.0 copy-done.1
  19.0 0.2 fusion.17
  19.2 0.3 copy.27
  19.5 0.2 reshape.21
  19.8 1.7 %convolution_convert_fusion = bf16[864,864]{1,0:T(8,128)(2,1)} fusion(bf16[864,64]{1,0:T(8,128)(2,1)S(1)} %reshape.21), kind=kOutput, calls=%fused_computation.8 | convolution fusion | flops 96297984 | bytes 1603584 | tf_op jit(solution)/shard_map/dot_general | solution.py:37
  21.5 0.0 reduce-scatter.2.cloned.1.call-update
  21.5 30.5 %reduce-scatter.2.cloned.1.call-done = bf16[432,864]{1,0:T(8,128)(2,1)} async-done(((bf16[864,864]{1,0:T(8,128)(2,1)}), bf16[432,864]{1,0:T(8,128)(2,1)}) %reduce-scatter.2.cloned.1.call-update) | async-done | bytes 746512 | tf_op jit(solution)/shard_map/reduce_scatter | solution.py:42
  51.9 74.4 %all-reduce.1 = f32[432,864]{1,0:T(8,128)S(1)} all-reduce(bf16[432,864]{1,0:T(8,128)(2,1)} %reduce-scatter.2.cloned.1.call-done), channel_id=1, replica_groups=mesh['vol'=2,'space'=16] {'space'}, use_global_device_ids=true, to_apply=%region_1.0 | all-reduce | flops 373248 | bytes 2239488 | tf_op jit(solution)/shard_map/psum | solution.py:45
  126.3 0.8 select_reduce_fusion
  127.8 5.5 %psum.15 = f32[]{:T(128)} all-reduce(f32[]{:T(128)} %select_reduce_fusion), channel_id=1, replica_groups=mesh['vol'=2,'space'=16] {'vol'}, use_global_device_ids=true, to_apply=%region_3.4 | all-reduce | flops 1 | bytes 8 | tf_op jit(solution)/shard_map/psum | solution.py:47
  134.0 8.6 %multiply_add_fusion = f32[432,864]{1,0:T(8,128)} fusion(f32[864,864]{1,0:T(8,128)} %param.8, s32[]{:T(128)S(6)} %select_n.9, f32[432,864]{1,0:T(8,128)S(1)} %all-reduce.1, f32[]{:T(128)S(6)} %mul.13), kind=kOutput, calls=%fused_computation.9 | convolution fusion | flops 3870955008 | bytes 7630856 | tf_op jit(solution)/shard_map/dot_general | solution.py:51
  (1 shorter events, 0.0 us)
Async XLA Ops:
  6.5 6.7 %copy-start = (bf16[32,32,3,3,3]{1,0,4,3,2:T(8,128)(2,1)S(1)}, bf16[32,32,3,3,3]{1,0,4,3,2:T(8,128)(2,1)}, u32[]{:S(2)}) copy-start(bf16[32,32,3,3,3]{1,0,4,3,2:T(8,128)(2,1)} %param.6) | copy-start | bytes 165892
  6.5 45.4 %reduce-scatter.2.cloned.1.call-start = ((), (), s32[]{:S(2)}) async-start(), calls=%async_computation.1 | async-start | bytes 2322432 | tf_op jit(solution)/shard_map/reduce_scatter | solution.py:42
  7.4 3.1 %collective-permute-start = (bf16[32,1,8,128]{3,2,1,0:T(8,128)(2,1)S(1)}, bf16[32,1,8,128]{3,2,1,0:T(8,128)(2,1)S(1)}, u32[]{:S(2)}, u32[]{:S(2)}) collective-permute-start(bf16[32,1,8,128]{3,2,1,0:T(8,128)(2,1)S(1)} %slice.10), channel_id=1, source_target_pairs={{1,0},{2,1},{3,2},{4,3},{5,4},{6,5},{7,6},{8,7},{9,8},{10,9},{11,1... | collective-permute-start | bytes 196616 | tf_op jit(solution)/shard_map/ppermute | solution.py:10
  12.9 0.7 copy-start.2
  18.0 1.0 copy-start.1
Sparse Core Ops, SparseCore 0:
  21.6 30.2 reduce-scatter.1
where the time goes:
time: 150 us; the launch traced here: 149 us
  blocking collectives  79.9 us (53%)
  waiting for transfers between devices  32.3 us (22%)
  between operations  14.9 us (10%)
  matrix products  14.1 us (9%)
  local copies, waits for them, and re-layouts  4.89 us (3%)
  other arithmetic  2.03 us (1%)
    psum x1, blocking collectives, body(): row_panel = lax.psum(partial_rows, 'space')  74.4 us
    reduce_scatter x1, waiting for transfers between devices, body(): lax.psum_scatter(local_gram.astype(jnp.bfloat16), 'vol', scatter_dimensio...  30.5 us
    dot_general x1, matrix products, body(): jnp.dot(normed_panel, basis, precision=lax.Precision.HIGHEST, preferred_e...  8.56 us
    psum x1, blocking collectives, body(): trace_value = lax.psum(jnp.trace(diag_block), 'vol')  5.53 us
    conv_general_dilated x1, matrix products, body(): lax.conv_general_dilated(stacked[None], conv_weight, (1, 1, 1), [(0, 0),...  3.85 us
  transfers between devices with their start and end apart: 2, of which 2 were waited for; matrix products, arithmetic and copies ran while one was open for 0% of the time, Pallas kernels for 0%

commit v1 on v0

--- a/solution.py
+++ b/solution.py
@@ -1,7 +1,14 @@
+import functools
+
 import jax
 import jax.numpy as jnp
 from jax import lax
+from jax.experimental import pallas as pl
+from jax.experimental.pallas import tpu as pltpu
 from jax.sharding import PartitionSpec as P
+
+MESH = pl.DeviceIdType.MESH
+GATHER_LIMIT = 8 << 20
 
 
 def shifted(block, axis, distance):
@@ -10,16 +17,14 @@
     return lax.ppermute(block, axis, route)
 
 
-def extract_patches(activated):
+def split_patches(activated):
     chans, planes, rows_y, cols_z = activated.shape
-    viewed = activated.reshape(chans, planes // 4, 4, rows_y // 4, 4, cols_z // 4, 4)[
+    return activated.reshape(chans, planes // 4, 4, rows_y // 4, 4, cols_z // 4, 4)[
         :, :, 1:, :, 1:, :, 1:
     ]
-    viewed = viewed.transpose(0, 2, 4, 6, 1, 3, 5)
-    return viewed.reshape(chans * 27, -1)
-
-
-def body(volume, conv_weight, conv_bias, basis, damping):
+
+
+def conv_block(volume, conv_weight, conv_bias):
     local_block = volume[0]
     from_above = shifted(local_block[:, 0:1], "space", -1)
     zero_plane = jnp.zeros_like(from_above)
@@ -32,8 +37,12 @@
         dimension_numbers=("NCDHW", "OIDHW", "NCDHW"),
         preferred_element_type=jnp.float32,
     )[0]
-    activated = jnp.maximum(conv_out + conv_bias[:, None, None, None], 0.0).astype(jnp.bfloat16)
-    patch_cols = extract_patches(activated)
+    return jnp.maximum(conv_out + conv_bias[:, None, None, None], 0.0).astype(jnp.bfloat16)
+
+
+def body_collective(volume, conv_weight, conv_bias, basis, damping):
+    viewed = split_patches(conv_block(volume, conv_weight, conv_bias))
+    patch_cols = viewed.transpose(0, 2, 4, 6, 1, 3, 5).reshape(viewed.shape[0] * 27, -1)
     local_gram = jnp.dot(patch_cols, patch_cols.T, preferred_element_type=jnp.float32)
     gram_width = local_gram.shape[0]
     total_patches = patch_cols.shape[1] * lax.axis_size("space") * lax.axis_size("vol")
@@ -54,6 +63,218 @@
     return product + damping[0] * mean_diagonal * basis_rows
 
 
+def gather_kernel(
+    nz, total, own_ref, basis_hbm, damping_ref, out_ref,
+    buf, acc, square, basis_f32, basis_hi, basis_lo,
+    basis_sem, z_send, x_send, y_send, a_send, b_send, c_send,
+    z_recv, x_recv, y_recv, a_recv, b_recv, c_recv,
+):
+    vol = lax.axis_index("vol")
+    space = lax.axis_index("space")
+    z = space // 4
+    here = (vol, space)
+    core_peer = (vol, space + 1 - 2 * lax.rem(space, 2))
+    x_peer = (vol, space + 2 - 4 * lax.rem(space // 2, 2))
+    y_peer = (1 - vol, space)
+    up_peer, down_peer = (vol, space + 4), (vol, space - 4)
+    patches, padded = own_ref.shape
+    half = patches // 2
+    panel, width = out_ref.shape
+
+    basis_copy = pltpu.make_async_copy(basis_hbm, basis_f32, basis_sem)
+    basis_copy.start()
+
+    barrier = pltpu.get_barrier_semaphore()
+    for peer in (core_peer, x_peer, y_peer):
+        pl.semaphore_signal(barrier, inc=1, device_id=peer, device_id_type=MESH)
+
+    @pl.when(z + 1 < nz)
+    def _():
+        pl.semaphore_signal(barrier, inc=1, device_id=up_peer, device_id_type=MESH)
+
+    @pl.when(z > 0)
+    def _():
+        pl.semaphore_signal(barrier, inc=1, device_id=down_peer, device_id_type=MESH)
+
+    buf[0, 0, z] = own_ref[...]
+    edges = jnp.where(z > 0, 1, 0) + jnp.where(z + 1 < nz, 1, 0)
+    pl.semaphore_wait(barrier, 3 + edges)
+
+    def remote(src, dst, send, recv, peer):
+        return pltpu.make_async_remote_copy(
+            src_ref=src, dst_ref=dst, send_sem=send, recv_sem=recv,
+            device_id=peer, device_id_type=MESH,
+        )
+
+    def z_copy(k, peer, way):
+        return remote(buf.at[0, 0, k], buf.at[0, 0, k], z_send.at[way, k], z_recv.at[k], peer)
+
+    def x_copy(k):
+        return remote(buf.at[0, 0, k], buf.at[0, 1, k], x_send.at[k], x_recv.at[k], x_peer)
+
+    def y_copy(k):
+        return remote(buf.at[0, 0, k], buf.at[0, 2, k], y_send.at[k], y_recv.at[k], y_peer)
+
+    def a_copy(k):
+        rows = pl.ds(0, half)
+        return remote(
+            buf.at[0, 1, k, rows], buf.at[0, 3, k, rows], a_send.at[k], a_recv.at[k], y_peer
+        )
+
+    def b_copy(k):
+        rows = pl.ds(half, half)
+        return remote(
+            buf.at[0, 2, k, rows], buf.at[0, 3, k, rows], b_send.at[k], b_recv.at[k], x_peer
+        )
+
+    def c_copy(q, k):
+        return remote(
+            buf.at[0, q, k], buf.at[1, q, k], c_send.at[q, k], c_recv.at[q, k], core_peer
+        )
+
+    def spread(k):
+        x_copy(k).start()
+        y_copy(k).start()
+        c_copy(0, k).start()
+
+    def relay(k):
+        x_copy(k).wait_recv()
+        a_copy(k).start()
+        c_copy(1, k).start()
+        y_copy(k).wait_recv()
+        b_copy(k).start()
+        c_copy(2, k).start()
+
+    def finish(k):
+        a_copy(k).wait_recv()
+        b_copy(k).wait_recv()
+        c_copy(3, k).start()
+
+    def both(s, action):
+        if s == 0:
+            action(z)
+            return
+        pl.when(z >= s)(lambda: action(z - s))
+        pl.when(z + s < nz)(lambda: action(z + s))
+
+    def gram(c, q):
+        block = buf[c, q].reshape(nz * patches, padded)
+        turned = block.T
+        wide = block.astype(jnp.float32)
+        sums = jnp.sum((wide * wide).reshape(-1, 8, padded), axis=0)
+        rows = jnp.where(vol == 0, turned[:panel], turned[panel : 2 * panel])
+        term = jnp.dot(rows, block, preferred_element_type=jnp.float32)
+        if c == 0 and q == 0:
+            acc[...] = term
+            square[...] = sums
+        else:
+            acc[...] += term
+            square[...] += sums
+
+    pl.when(z + 1 < nz)(lambda: z_copy(z, up_peer, 0).start())
+    pl.when(z > 0)(lambda: z_copy(z, down_peer, 1).start())
+    spread(z)
+
+    basis_copy.wait()
+    basis_hi[...] = basis_f32[...].astype(jnp.bfloat16)
+    basis_lo[...] = (basis_f32[...] - basis_hi[...].astype(jnp.float32)).astype(jnp.bfloat16)
+
+    for s in range(1, nz):
+        @pl.when(z >= s)
+        def _():
+            k = z - s
+            z_copy(k, up_peer, 0).wait_recv()
+            pl.when(z + 1 < nz)(lambda: z_copy(k, up_peer, 0).start())
+            spread(k)
+
+        @pl.when(z + s < nz)
+        def _():
+            k = z + s
+            z_copy(k, down_peer, 1).wait_recv()
+            pl.when(z > 0)(lambda: z_copy(k, down_peer, 1).start())
+            spread(k)
+
+        both(s - 1, relay)
+    gram(0, 0)
+    both(nz - 1, relay)
+    for s in range(nz):
+        both(s, finish)
+    for q in range(4):
+        if q > 0:
+            gram(0, q)
+        for k in range(nz):
+            c_copy(q, k).wait_recv()
+        gram(1, q)
+
+    scale = 1.0 / total
+    mean_diag = jnp.sum(square[...]) * (scale / width)
+    value = acc[:, :width]
+    high = value.astype(jnp.bfloat16)
+    low = (value - high.astype(jnp.float32)).astype(jnp.bfloat16)
+    product = jnp.dot(high, basis_hi[...], preferred_element_type=jnp.float32)
+    product += jnp.dot(high, basis_lo[...], preferred_element_type=jnp.float32)
+    product += jnp.dot(low, basis_hi[...], preferred_element_type=jnp.float32)
+    basis_rows = basis_f32[pl.ds(pl.multiple_of(vol * panel, 16), panel), :]
+    out_ref[...] = product * scale + (damping_ref[0] * mean_diag) * basis_rows
+
+    for k in range(nz):
+        pl.when((z + 1 < nz) & (k <= z))(lambda: z_copy(k, up_peer, 0).wait_send())
+        pl.when((z > 0) & (k >= z))(lambda: z_copy(k, down_peer, 1).wait_send())
+        x_copy(k).wait_send()
+        y_copy(k).wait_send()
+        a_copy(k).wait_send()
+        b_copy(k).wait_send()
+        for q in range(4):
+            c_copy(q, k).wait_send()
+
+
+def body_gather(volume, conv_weight, conv_bias, basis, damping):
+    viewed = split_patches(conv_block(volume, conv_weight, conv_bias))
+    width = viewed.shape[0] * 27
+    own = viewed.transpose(1, 3, 5, 0, 2, 4, 6).reshape(-1, width)
+    patches = own.shape[0]
+    padded = -(-width // 128) * 128
+    own = jnp.pad(own, ((0, 0), (0, padded - width)))
+    space = lax.axis_size("space")
+    nz = space // 4
+    panel = width // lax.axis_size("vol")
+    total = patches * space * lax.axis_size("vol")
+    dma = pltpu.SemaphoreType.DMA
+    return pl.pallas_call(
+        functools.partial(gather_kernel, nz, total),
+        out_shape=jax.ShapeDtypeStruct((panel, width), jnp.float32),
+        in_specs=[
+            pl.BlockSpec(memory_space=pltpu.VMEM),
+            pl.BlockSpec(memory_space=pl.ANY),
+            pl.BlockSpec(memory_space=pltpu.SMEM),
+        ],
+        out_specs=pl.BlockSpec(memory_space=pltpu.VMEM),
+        scratch_shapes=[
+            pltpu.VMEM((2, 4, nz, patches, padded), jnp.bfloat16),
+            pltpu.VMEM((panel, padded), jnp.float32),
+            pltpu.VMEM((8, padded), jnp.float32),
+            pltpu.VMEM((width, width), jnp.float32),
+            pltpu.VMEM((width, width), jnp.bfloat16),
+            pltpu.VMEM((width, width), jnp.bfloat16),
+            dma,
+            dma((2, nz)), dma((nz,)), dma((nz,)), dma((nz,)), dma((nz,)), dma((4, nz)),
+            dma((nz,)), dma((nz,)), dma((nz,)), dma((nz,)), dma((nz,)), dma((4, nz)),
+        ],
+        compiler_params=pltpu.CompilerParams(
+            collective_id=0, has_side_effects=True, vmem_limit_bytes=48 << 20
+        ),
+    )(own, basis, damping)
+
+
+def body(volume, conv_weight, conv_bias, basis, damping):
+    vol, space = lax.axis_size("vol"), lax.axis_size("space")
+    cells = volume.shape[2] * volume.shape[3] * volume.shape[4]
+    gathered = 2 * volume.shape[1] * 27 * (cells // 64) * vol * space
+    if vol == 2 and space % 4 == 0 and gathered <= GATHER_LIMIT:
+        return body_gather(volume, conv_weight, conv_bias, basis, damping)
+    return body_collective(volume, conv_weight, conv_bias, basis, damping)
+
+
 def solution(mesh):
     in_specs = (P("vol", None, "space", None, None), P(), P(), P(), P())
     out_specs = P("vol", None)

time: 150 us -> 70.3 us (0.47)
  blocking collectives: 79.9 us -> 0 us
  Pallas kernels: 0 us -> 33.1 us
  waiting for transfers between devices: 32.3 us -> 1.19 us
  between operations: 14.9 us -> 0.73 us
  local copies, waits for them, and re-layouts: 4.89 us -> 14.2 us
  matrix products: 14.1 us -> 16.2 us
    psum x2 -> x0, blocking collectives: 79.9 us -> none  [the longest x1 74.4 us: body(): row_panel = lax.psum(partial_rows, 'space')]
    pallas_call x0 -> x1, Pallas kernels: none -> 33.1 us  [body_gather(): pl.pallas_call(functools.partial(gather_kernel, nz, total), out_shape=jax...]
    reduce_scatter x1 -> x0, waiting for transfers between devices: 30.5 us -> none  [body(): lax.psum_scatter(local_gram.astype(jnp.bfloat16), 'vol', scatter_dimensio...]
    conv_general_dilated x1, matrix products: 3.85 us -> 16.2 us  [conv_block(): lax.conv_general_dilated(stacked[None], conv_weight, (1, 1, 1), [(0, 0),...]
    dot_general x2 -> x0, matrix products: 10.3 us -> none  [the longest x1 8.56 us: body(): jnp.dot(normed_panel, basis, precision=lax.Precision.HIGHEST, preferred_e...]
    broadcast_in_dim x1, local copies, waits for them, and re-layouts: 0.31 us -> 4.37 us  [conv_block(): stacked[None]]
    unnamed x7 -> x8, local copies, waits for them, and re-layouts: 1.01 us -> 3.52 us
    reshape x1 -> x2, local copies, waits for them, and re-layouts: 0.24 us -> 2.05 us  [body_gather(): own = viewed.transpose(1, 3, 5, 0, 2, 4, 6).reshape(-1, width)]
  transfers between devices with their start and end apart: 2 -> 1, of which waited for: 2 -> 1; matrix products, arithmetic and copies ran while one was open for 0% -> 0% of each run, Pallas kernels for 0% -> 0%
where the time goes in v1:
time: 70.3 us; the launch traced here: 69.8 us
  Pallas kernels  33.1 us (47%)
  matrix products  16.2 us (23%)
  local copies, waits for them, and re-layouts  14.2 us (20%)
  other arithmetic  3.13 us (4%)
  starting transfers between devices  1.28 us (2%)
  waiting for transfers between devices  1.19 us (2%)
  between operations  0.73 us (1%)
    pallas_call x1, Pallas kernels, body_gather(): pl.pallas_call(functools.partial(gather_kernel, nz, total), out_shape=jax...  33.1 us
    conv_general_dilated x1, matrix products, conv_block(): lax.conv_general_dilated(stacked[None], conv_weight, (1, 1, 1), [(0, 0),...  16.2 us
    broadcast_in_dim x1, local copies, waits for them, and re-layouts, conv_block(): stacked[None]  4.37 us
    unnamed x8, local copies, waits for them, and re-layouts  3.52 us
    reshape x2, local copies, waits for them, and re-layouts, body_gather(): own = viewed.transpose(1, 3, 5, 0, 2, 4, 6).reshape(-1, width)  2.05 us
    broadcast_in_dim x1, other arithmetic, conv_block(): stacked[None]  1.8 us
  transfers between devices with their start and end apart: 1, of which 1 were waited for; matrix products, arithmetic and copies ran while one was open for 0% of the time, Pallas kernels for 0%

profile of v1, /device:TPU:0, one launch (start us, length us, event | category | flops | bytes accessed | tf_op | source)
XLA Modules:
  0.0 69.8 jit_solution(4011670888257194525)
XLA Ops:
  0.0 0.0 copy-start
  0.0 0.9 %slice.8 = bf16[32,1,8,128]{3,2,1,0:T(8,128)(2,1)S(1)} slice(bf16[32,4,8,128]{3,2,1,0:T(8,128)(2,1)} %bitcast.12), slice={[0:32], [0:1], [0:8], [0:128]} | slice | bytes 131072 | tf_op jit(solution)/shard_map/slice | solution.py:29
  0.9 1.3 %collective-permute-start = (bf16[32,1,8,128]{3,2,1,0:T(8,128)(2,1)S(1)}, bf16[32,1,8,128]{3,2,1,0:T(8,128)(2,1)S(1)}, u32[]{:S(2)}, u32[]{:S(2)}) collective-permute-start(bf16[32,1,8,128]{3,2,1,0:T(8,128)(2,1)S(1)} %slice.8), channel_id=1, source_target_pairs={{1,0},{2,1},{3,2},{4,3},{5,4},{6,5},{7,6},{8,7},{9,8},{10,9},{11,1... | collective-permute-start | bytes 196616 | tf_op jit(solution)/shard_map/ppermute | solution.py:17
  2.8 1.2 %collective-permute-done = bf16[32,1,8,128]{3,2,1,0:T(8,128)(2,1)S(1)} collective-permute-done((bf16[32,1,8,128]{3,2,1,0:T(8,128)(2,1)S(1)}, bf16[32,1,8,128]{3,2,1,0:T(8,128)(2,1)S(1)}, u32[]{:S(2)}, u32[]{:S(2)}) %collective-permute-start) | collective-permute-done | bytes 65568 | tf_op jit(solution)/shard_map/ppermute | solution.py:17
  4.0 1.8 %maximum_bitcast_fusion = bf16[1,32,6,8,128]{4,3,2,1,0:T(8,128)(2,1)} fusion(bf16[32,1,8,128]{3,2,1,0:T(8,128)(2,1)S(1)} %collective-permute-done, bf16[32,4,8,128]{3,2,1,0:T(8,128)(2,1)} %bitcast.13, bf16[6]{0:T(256)(128)(2,1)S(1)} %pad.5.clone), kind=kLoop, calls=%fused_computation.2 | loop fusion | flops 393216 | bytes 720908 | tf_op jit(solution)/shard_map/broadcast_in_dim | solution.py:33
  5.8 4.4 %copy.14 = bf16[1,32,6,8,128]{1,0,4,3,2:T(2,128)(2,1)S(1)} copy(bf16[1,32,6,8,128]{4,3,2,1,0:T(8,128)(2,1)} %maximum_bitcast_fusion) | data formatting | bytes 786432 | tf_op jit(solution)/shard_map/broadcast_in_dim | solution.py:33
  10.2 0.0 copy-done
  10.2 16.2 %fusion.1 = f32[1,32,4,8,128]{1,0,4,3,2:T(1,128)S(1)} fusion(bf16[1,32,6,8,128]{1,0,4,3,2:T(2,128)(2,1)S(1)} %copy.14, bf16[32,32,3,3,3]{1,0,4,3,2:T(8,128)(2,1)S(1)} %copy-done), kind=kOutput, calls=%fused_computation.3 | convolution fusion | flops 206536704 | bytes 972800 | tf_op jit(solution)/shard_map/conv_general_dilated | solution.py:32
  26.4 0.0 copy-start.2
  26.4 1.3 %slice.9 = f32[32,1,3,2,3,32,3]{0,6,5,4,3,2,1:T(4,128)} slice(f32[32,1,4,2,4,32,4]{0,6,5,4,3,2,1:T(4,128)S(1)} %bitcast.11), slice={[0:32], [0:1], [1:4], [0:2], [1:4], [0:32], [1:4]} | slice | bytes 442368 | tf_op jit(solution)/shard_map/slice | solution.py:22
  27.8 0.0 copy-start.1
  27.8 2.4 %copy.18 = f32[32,1,3,2,3,32,3]{5,0,6,4,3,2,1:T(8,128)} copy(f32[32,1,3,2,3,32,3]{0,6,5,4,3,2,1:T(4,128)} %slice.9) | data formatting | bytes 442368
  30.1 0.0 copy-done.2
  30.1 1.3 %fusion = bf16[1,2,32,32,3,3,3]{2,3,6,5,1,4,0:T(8,128)(2,1)S(1)} fusion(f32[32,1,3,2,3,32,3]{5,0,6,4,3,2,1:T(8,128)} %copy.18, f32[32]{0:T(128)S(1)} %copy-done.2), kind=kLoop, calls=%fused_computation.1 | loop fusion | flops 165888 | bytes 331904 | tf_op jit(solution)/shard_map/transpose | solution.py:234
  31.5 1.1 %copy.16 = bf16[1,2,32,32,3,3,3]{2,1,6,5,4,3,0:T(2,128)(2,1)} copy(bf16[1,2,32,32,3,3,3]{2,3,6,5,1,4,0:T(8,128)(2,1)S(1)} %fusion) | data formatting | bytes 221184 | tf_op jit(solution)/shard_map/transpose | solution.py:234
  32.6 1.3 %reshape.21 = bf16[64,864]{0,1:T(8,128)(2,1)S(1)} reshape(bf16[1,2,32,32,3,3,3]{2,1,6,5,4,3,0:T(2,128)(2,1)} %copy.16) | data formatting | bytes 221184 | tf_op jit(solution)/shard_map/reshape | solution.py:234
  33.9 0.8 %copy.17 = bf16[64,864]{1,0:T(8,128)(2,1)} copy(bf16[64,864]{0,1:T(8,128)(2,1)S(1)} %reshape.21) | data formatting | bytes 221184 | tf_op jit(solution)/shard_map/reshape | solution.py:234
  34.6 0.9 %pad.4.own_ref = bf16[64,896]{1,0:T(8,128)(2,1)S(1)} pad(bf16[64,864]{1,0:T(8,128)(2,1)} %copy.17, bf16[]{:T(256)} %constant.2.clone.1), padding=0_0x0_32 | pad | bytes 225282 | tf_op jit(solution)/shard_map/jit(_pad)/pad | solution.py:237
  35.6 0.0 copy-done.1
  35.6 33.1 %shard_map.55 = f32[432,864]{1,0:T(8,128)S(1)} custom-call(bf16[64,896]{1,0:T(8,128)(2,1)S(1)} %pad.4.own_ref, f32[864,864]{1,0:T(8,128)S(1)} %copy-done.1, f32[1]{0:T(128)S(6)} %copy.20.damping_ref), custom_call_target="tpu_custom_call" | custom-call | tf_op jit(solution)/shard_map/pallas_call | solution.py:243
  68.6 1.1 %copy.21 = f32[432,864]{1,0:T(8,128)} copy(f32[432,864]{1,0:T(8,128)S(1)} %shard_map.55) | data formatting | bytes 2985984
  (1 shorter events, 0.0 us)
Async XLA Ops:
  0.0 10.2 %copy-start = (bf16[32,32,3,3,3]{1,0,4,3,2:T(8,128)(2,1)S(1)}, bf16[32,32,3,3,3]{1,0,4,3,2:T(8,128)(2,1)}, u32[]{:S(2)}) copy-start(bf16[32,32,3,3,3]{1,0,4,3,2:T(8,128)(2,1)} %param.6) | copy-start | bytes 165892
  0.9 3.1 %collective-permute-start = (bf16[32,1,8,128]{3,2,1,0:T(8,128)(2,1)S(1)}, bf16[32,1,8,128]{3,2,1,0:T(8,128)(2,1)S(1)}, u32[]{:S(2)}, u32[]{:S(2)}) collective-permute-start(bf16[32,1,8,128]{3,2,1,0:T(8,128)(2,1)S(1)} %slice.8), channel_id=1, source_target_pairs={{1,0},{2,1},{3,2},{4,3},{5,4},{6,5},{7,6},{8,7},{9,8},{10,9},{11,1... | collective-permute-start | bytes 196616 | tf_op jit(solution)/shard_map/ppermute | solution.py:17
  26.4 3.7 %copy-start.2 = (f32[32]{0:T(128)S(1)}, f32[32]{0:T(128)}, u32[]{:S(2)}) copy-start(f32[32]{0:T(128)} %param.7) | copy-start | bytes 388
  27.8 7.8 %copy-start.1 = (f32[864,864]{1,0:T(8,128)S(1)}, f32[864,864]{1,0:T(8,128)}, u32[]{:S(2)}) copy-start(f32[864,864]{1,0:T(8,128)} %basis_hbm.1) | copy-start | bytes 8957956

commit v2 on v1

--- a/solution.py
+++ b/solution.py
@@ -63,10 +63,77 @@
     return product + damping[0] * mean_diagonal * basis_rows
 
 
+def wait_halo(present, halo_copy, halo):
+    @pl.when(present)
+    def _():
+        halo_copy().wait_recv()
+
+    @pl.when(jnp.logical_not(present))
+    def _():
+        halo[...] = jnp.zeros_like(halo)
+
+
+def own_patches(
+    cells_ref, weight_ref, bias_ref, halo, taps, partial, active, padded, wait
+):
+    planes, rows_y, chans, cols_z = cells_ref.shape
+    out_rows = [y for y in range(rows_y) if y % 4]
+    lane = lax.broadcasted_iota(jnp.int32, (rows_y * chans, cols_z), 1)
+
+    def plane(p, cells):
+        wide = cells.astype(jnp.float32).reshape(rows_y * chans, cols_z)
+        left = jnp.where(lane == 0, 0.0, pltpu.roll(wide, 1, 1))
+        right = jnp.where(lane == cols_z - 1, 0.0, pltpu.roll(wide, cols_z - 1, 1))
+        for d, moved in enumerate((left, wide, right)):
+            taps[0:rows_y, d] = moved.astype(jnp.bfloat16).reshape(rows_y, chans, cols_z)
+        taps[rows_y] = jnp.zeros_like(taps[rows_y])
+        for n, y in enumerate(out_rows):
+            window = taps[y - 1 : y + 2].reshape(9 * chans, cols_z)
+            partial[p, n] = jnp.dot(
+                weight_ref[...], window, preferred_element_type=jnp.float32
+            )
+
+    for p in range(planes):
+        plane(p, cells_ref[p])
+
+    source = lax.broadcasted_iota(jnp.int32, (9 * chans, padded), 0)
+    target = lax.broadcasted_iota(jnp.int32, (9 * chans, padded), 1)
+    target -= (source % chans) * 27 + (source // chans) * 3
+    order = [jnp.where(target == c, 1.0, 0.0).astype(jnp.bfloat16) for c in range(3)]
+    ks = cols_z // 4
+    row = lax.broadcasted_iota(jnp.int32, (3 * ks, cols_z), 0)
+    col = lax.broadcasted_iota(jnp.int32, (3 * ks, cols_z), 1)
+    pick = jnp.where(col == 4 * (row % ks) + row // ks + 1, 1.0, 0.0).astype(jnp.bfloat16)
+
+    wait()
+    plane(planes, halo[...])
+
+    picked = []
+    for j in range(rows_y // 4):
+        for a in range(3):
+            for b in range(3):
+                n = 3 * j + b
+                value = partial[a, n, 0:chans] + partial[a + 1, n, chans : 2 * chans]
+                value += partial[a + 2, n, 2 * chans : 3 * chans]
+                value = jnp.maximum(value + bias_ref[...], 0.0).astype(jnp.bfloat16)
+                active[(3 * a + b) * chans : (3 * a + b + 1) * chans] = value
+        picked.append(
+            lax.dot_general(
+                pick, active[...], (((1,), (1,)), ((), ())), preferred_element_type=jnp.float32
+            ).astype(jnp.bfloat16)
+        )
+    total = None
+    for c in range(3):
+        part = jnp.concatenate([x[c * ks : (c + 1) * ks] for x in picked], axis=0)
+        term = jnp.dot(part, order[c], preferred_element_type=jnp.float32)
+        total = term if total is None else total + term
+    return total.astype(jnp.bfloat16)
+
+
 def gather_kernel(
-    nz, total, own_ref, basis_hbm, damping_ref, out_ref,
-    buf, acc, square, basis_f32, basis_hi, basis_lo,
-    basis_sem, z_send, x_send, y_send, a_send, b_send, c_send,
+    nz, total, cells_ref, weight_ref, bias_ref, basis_hbm, damping_ref, out_ref,
+    halo, taps, partial, active, buf, acc, square, basis_f32, basis_hi, basis_lo,
+    basis_sem, halo_send, halo_recv, z_send, x_send, y_send, a_send, b_send, c_send,
     z_recv, x_recv, y_recv, a_recv, b_recv, c_recv,
 ):
     vol = lax.axis_index("vol")
@@ -77,7 +144,8 @@
     x_peer = (vol, space + 2 - 4 * lax.rem(space // 2, 2))
     y_peer = (1 - vol, space)
     up_peer, down_peer = (vol, space + 4), (vol, space - 4)
-    patches, padded = own_ref.shape
+    patches, padded = buf.shape[3:]
+    ends = lax.axis_size("space")
     half = patches // 2
     panel, width = out_ref.shape
 
@@ -96,8 +164,16 @@
     def _():
         pl.semaphore_signal(barrier, inc=1, device_id=down_peer, device_id_type=MESH)
 
-    buf[0, 0, z] = own_ref[...]
+    @pl.when(space > 0)
+    def _():
+        pl.semaphore_signal(barrier, inc=1, device_id=(vol, space - 1), device_id_type=MESH)
+
+    @pl.when(space + 1 < ends)
+    def _():
+        pl.semaphore_signal(barrier, inc=1, device_id=(vol, space + 1), device_id_type=MESH)
+
     edges = jnp.where(z > 0, 1, 0) + jnp.where(z + 1 < nz, 1, 0)
+    edges += jnp.where(space > 0, 1, 0) + jnp.where(space + 1 < ends, 1, 0)
     pl.semaphore_wait(barrier, 3 + edges)
 
     def remote(src, dst, send, recv, peer):
@@ -105,6 +181,15 @@
             src_ref=src, dst_ref=dst, send_sem=send, recv_sem=recv,
             device_id=peer, device_id_type=MESH,
         )
+
+    def halo_copy():
+        return remote(cells_ref.at[0], halo, halo_send, halo_recv, (vol, space - 1))
+
+    pl.when(space > 0)(lambda: halo_copy().start())
+    buf[0, 0, z] = own_patches(
+        cells_ref, weight_ref, bias_ref, halo, taps, partial, active, padded,
+        lambda: wait_halo(space + 1 < ends, halo_copy, halo),
+    )
 
     def z_copy(k, peer, way):
         return remote(buf.at[0, 0, k], buf.at[0, 0, k], z_send.at[way, k], z_recv.at[k], peer)
@@ -217,6 +302,7 @@
     basis_rows = basis_f32[pl.ds(pl.multiple_of(vol * panel, 16), panel), :]
     out_ref[...] = product * scale + (damping_ref[0] * mean_diag) * basis_rows
 
+    pl.when(space > 0)(lambda: halo_copy().wait_send())
     for k in range(nz):
         pl.when((z + 1 < nz) & (k <= z))(lambda: z_copy(k, up_peer, 0).wait_send())
         pl.when((z > 0) & (k >= z))(lambda: z_copy(k, down_peer, 1).wait_send())
@@ -229,12 +315,12 @@
 
 
 def body_gather(volume, conv_weight, conv_bias, basis, damping):
-    viewed = split_patches(conv_block(volume, conv_weight, conv_bias))
-    width = viewed.shape[0] * 27
-    own = viewed.transpose(1, 3, 5, 0, 2, 4, 6).reshape(-1, width)
-    patches = own.shape[0]
+    chans, planes, rows_y, cols_z = volume.shape[1:]
+    width = chans * 27
+    patches = (planes // 4) * (rows_y // 4) * (cols_z // 4)
+    cells = volume[0].transpose(1, 2, 0, 3)
+    weight = conv_weight.transpose(2, 0, 3, 4, 1).reshape(3 * chans, 9 * chans)
     padded = -(-width // 128) * 128
-    own = jnp.pad(own, ((0, 0), (0, padded - width)))
     space = lax.axis_size("space")
     nz = space // 4
     panel = width // lax.axis_size("vol")
@@ -245,32 +331,39 @@
         out_shape=jax.ShapeDtypeStruct((panel, width), jnp.float32),
         in_specs=[
             pl.BlockSpec(memory_space=pltpu.VMEM),
-            pl.BlockSpec(memory_space=pl.ANY),
+            pl.BlockSpec(memory_space=pltpu.VMEM),
+            pl.BlockSpec(memory_space=pltpu.VMEM),
+            pl.BlockSpec(memory_space=pltpu.HBM),
             pl.BlockSpec(memory_space=pltpu.SMEM),
         ],
         out_specs=pl.BlockSpec(memory_space=pltpu.VMEM),
         scratch_shapes=[
+            pltpu.VMEM((rows_y, chans, cols_z), jnp.bfloat16),
+            pltpu.VMEM((rows_y + 1, 3, chans, cols_z), jnp.bfloat16),
+            pltpu.VMEM((planes + 1, 3 * rows_y // 4, 3 * chans, cols_z), jnp.float32),
+            pltpu.VMEM((9 * chans, cols_z), jnp.bfloat16),
             pltpu.VMEM((2, 4, nz, patches, padded), jnp.bfloat16),
             pltpu.VMEM((panel, padded), jnp.float32),
             pltpu.VMEM((8, padded), jnp.float32),
             pltpu.VMEM((width, width), jnp.float32),
             pltpu.VMEM((width, width), jnp.bfloat16),
             pltpu.VMEM((width, width), jnp.bfloat16),
-            dma,
+            dma, dma, dma,
             dma((2, nz)), dma((nz,)), dma((nz,)), dma((nz,)), dma((nz,)), dma((4, nz)),
             dma((nz,)), dma((nz,)), dma((nz,)), dma((nz,)), dma((nz,)), dma((4, nz)),
         ],
         compiler_params=pltpu.CompilerParams(
             collective_id=0, has_side_effects=True, vmem_limit_bytes=48 << 20
         ),
-    )(own, basis, damping)
+    )(cells, weight, conv_bias[:, None], basis, damping)
 
 
 def body(volume, conv_weight, conv_bias, basis, damping):
     vol, space = lax.axis_size("vol"), lax.axis_size("space")
     cells = volume.shape[2] * volume.shape[3] * volume.shape[4]
     gathered = 2 * volume.shape[1] * 27 * (cells // 64) * vol * space
-    if vol == 2 and space % 4 == 0 and gathered <= GATHER_LIMIT:
+    one_plane = volume.shape[2] == 4 and volume.shape[4] % 128 == 0
+    if one_plane and vol == 2 and space % 4 == 0 and gathered <= GATHER_LIMIT:
         return body_gather(volume, conv_weight, conv_bias, basis, damping)
     return body_collective(volume, conv_weight, conv_bias, basis, damping)
 

time: 70.3 us -> 40.7 us (0.58)
  matrix products: 16.2 us -> 0 us
  local copies, waits for them, and re-layouts: 14.2 us -> 6.08 us
  other arithmetic: 3.13 us -> 0 us
  starting transfers between devices: 1.28 us -> 0 us
  waiting for transfers between devices: 1.19 us -> 0 us
    conv_general_dilated x1 -> x0, matrix products: 16.2 us -> none  [conv_block(): lax.conv_general_dilated(stacked[None], conv_weight, (1, 1, 1), [(0, 0),...]
    broadcast_in_dim x1, local copies, waits for them, and re-layouts: 4.37 us -> 0.74 us  [body_gather(): conv_bias[:, None]]
    slice x2 -> x0, local copies, waits for them, and re-layouts: 2.21 us -> none  [the longest x1 1.33 us: split_patches(): activated.reshape(chans, planes // 4, 4, rows_y // 4, 4, cols_z // 4, 4)]
    reshape x2 -> x1, local copies, waits for them, and re-layouts: 2.05 us -> 0.19 us  [body_gather(): weight = conv_weight.transpose(2, 0, 3, 4, 1).reshape(3 * chans, 9 * chans)]
    broadcast_in_dim x1 -> x0, other arithmetic: 1.8 us -> none  [conv_block(): stacked[None]]
    transpose x1 -> x0, other arithmetic: 1.33 us -> none  [body_gather(): own = viewed.transpose(1, 3, 5, 0, 2, 4, 6).reshape(-1, width)]
    ppermute x1 -> x0, starting transfers between devices: 1.28 us -> none  [shifted(): return lax.ppermute(block, axis, route)]
    ppermute x1 -> x0, waiting for transfers between devices: 1.19 us -> none  [shifted(): return lax.ppermute(block, axis, route)]
  transfers between devices with their start and end apart: 1 -> 0, of which waited for: 1 -> 0; matrix products, arithmetic and copies ran while one was open for 0% -> 0% of each run, Pallas kernels for 0% -> 0%
where the time goes in v2:
time: 40.7 us; the launch traced here: 40.5 us
  Pallas kernels  33.7 us (83%)
  local copies, waits for them, and re-layouts  6.08 us (15%)
  between operations  0.67 us (2%)
    pallas_call x1, Pallas kernels, body_gather(): pl.pallas_call(functools.partial(gather_kernel, nz, total), out_shape=jax...  33.7 us
    unnamed x4, local copies, waits for them, and re-layouts  4.06 us
    transpose x1, local copies, waits for them, and re-layouts, body_gather(): weight = conv_weight.transpose(2, 0, 3, 4, 1).reshape(3 * chans, 9 * chans)  1.09 us

profile of v2, /device:TPU:0, one launch (start us, length us, event | category | flops | bytes accessed | tf_op | source)
XLA Modules:
  0.0 40.5 jit_solution(4489319809256403246)
XLA Ops:
  0.7 0.7 %copy.11.bias_ref = f32[32,1]{1,0:T(8,128)S(1)} copy(f32[32,1]{0,1:T(1,128)} %bitcast.9) | data formatting | bytes 256 | tf_op jit(solution)/shard_map/broadcast_in_dim | solution.py:358
  1.4 1.1 %copy.13 = bf16[1,32,4,8,128]{4,1,3,2,0:T(8,128)(2,1)S(1)} copy(bf16[1,32,4,8,128]{4,3,2,1,0:T(8,128)(2,1)} %param.5) | data formatting | bytes 524288 | tf_op args[0]
  2.4 1.1 %copy.10 = bf16[3,32,3,3,32]{4,3,2,1,0:T(4,128)(2,1)S(1)} copy(bf16[3,32,3,3,32]{4,1,3,2,0:T(8,128)(2,1)} %bitcast.8) | data formatting | bytes 110592 | tf_op jit(solution)/shard_map/transpose | solution.py:322
  3.5 0.2 reshape.3.weight_ref
  3.7 0.0 copy-start
  3.7 1.9 %copy-done = f32[864,864]{1,0:T(8,128)S(1)} copy-done((f32[864,864]{1,0:T(8,128)S(1)}, f32[864,864]{1,0:T(8,128)}, u32[]{:S(2)}) %copy-start) | copy-done | bytes 2986008
  5.6 33.7 %shard_map.55 = f32[432,864]{1,0:T(8,128)S(1)} custom-call(bf16[4,8,32,128]{3,2,1,0:T(8,128)(2,1)S(1)} %bitcast.7, bf16[96,288]{1,0:T(8,128)(2,1)S(1)} %reshape.3.weight_ref, f32[32,1]{1,0:T(8,128)S(1)} %copy.11.bias_ref, f32[864,864]{1,0:T(8,128)S(1)} %copy-done, f32[1]{0:T(128)S(6)} %copy.15.damping_ref), custom_call_target="tpu_custom_call" | custom-call | tf_op jit(solution)/shard_map/pallas_call | solution.py:329
  39.3 1.1 %copy.16 = f32[432,864]{1,0:T(8,128)} copy(f32[432,864]{1,0:T(8,128)S(1)} %shard_map.55) | data formatting | bytes 2985984
Async XLA Ops:
  3.7 1.9 %copy-start = (f32[864,864]{1,0:T(8,128)S(1)}, f32[864,864]{1,0:T(8,128)}, u32[]{:S(2)}) copy-start(f32[864,864]{1,0:T(8,128)} %basis_hbm.1) | copy-start | bytes 8957956

commit v3 on v2

--- a/solution.py
+++ b/solution.py
@@ -74,11 +74,16 @@
 
 
 def own_patches(
-    cells_ref, weight_ref, bias_ref, halo, taps, partial, active, padded, wait
+    cells_ref, weight_ref, bias_ref, halo, weights, taps, partial, active, padded, wait
 ):
     planes, rows_y, chans, cols_z = cells_ref.shape
     out_rows = [y for y in range(rows_y) if y % 4]
     lane = lax.broadcasted_iota(jnp.int32, (rows_y * chans, cols_z), 1)
+
+    for d in range(3):
+        weights[d * chans : (d + 1) * chans] = jnp.concatenate(
+            [weight_ref[9 * d + t].astype(jnp.float32) for t in range(9)], axis=1
+        ).astype(jnp.bfloat16)
 
     def plane(p, cells):
         wide = cells.astype(jnp.float32).reshape(rows_y * chans, cols_z)
@@ -90,7 +95,7 @@
         for n, y in enumerate(out_rows):
             window = taps[y - 1 : y + 2].reshape(9 * chans, cols_z)
             partial[p, n] = jnp.dot(
-                weight_ref[...], window, preferred_element_type=jnp.float32
+                weights[...], window, preferred_element_type=jnp.float32
             )
 
     for p in range(planes):
@@ -105,6 +110,12 @@
     col = lax.broadcasted_iota(jnp.int32, (3 * ks, cols_z), 1)
     pick = jnp.where(col == 4 * (row % ks) + row // ks + 1, 1.0, 0.0).astype(jnp.bfloat16)
 
+    square = (chans, chans)
+    diagonal = lax.broadcasted_iota(jnp.int32, square, 0) == lax.broadcasted_iota(
+        jnp.int32, square, 1
+    )
+    bias = jnp.sum(jnp.where(diagonal, bias_ref[...], 0.0), axis=1, keepdims=True)
+
     wait()
     plane(planes, halo[...])
 
@@ -115,7 +126,7 @@
                 n = 3 * j + b
                 value = partial[a, n, 0:chans] + partial[a + 1, n, chans : 2 * chans]
                 value += partial[a + 2, n, 2 * chans : 3 * chans]
-                value = jnp.maximum(value + bias_ref[...], 0.0).astype(jnp.bfloat16)
+                value = jnp.maximum(value + bias, 0.0).astype(jnp.bfloat16)
                 active[(3 * a + b) * chans : (3 * a + b + 1) * chans] = value
         picked.append(
             lax.dot_general(
@@ -132,7 +143,7 @@
 
 def gather_kernel(
     nz, total, cells_ref, weight_ref, bias_ref, basis_hbm, damping_ref, out_ref,
-    halo, taps, partial, active, buf, acc, square, basis_f32, basis_hi, basis_lo,
+    halo, weights, taps, partial, active, buf, acc, square, basis_f32, basis_hi, basis_lo,
     basis_sem, halo_send, halo_recv, z_send, x_send, y_send, a_send, b_send, c_send,
     z_recv, x_recv, y_recv, a_recv, b_recv, c_recv,
 ):
@@ -187,7 +198,7 @@
 
     pl.when(space > 0)(lambda: halo_copy().start())
     buf[0, 0, z] = own_patches(
-        cells_ref, weight_ref, bias_ref, halo, taps, partial, active, padded,
+        cells_ref, weight_ref, bias_ref, halo, weights, taps, partial, active, padded,
         lambda: wait_halo(space + 1 < ends, halo_copy, halo),
     )
 
@@ -280,16 +291,25 @@
             spread(k)
 
         both(s - 1, relay)
-    gram(0, 0)
     both(nz - 1, relay)
-    for s in range(nz):
-        both(s, finish)
-    for q in range(4):
-        if q > 0:
-            gram(0, q)
+
+    def other_core(q):
         for k in range(nz):
             c_copy(q, k).wait_recv()
         gram(1, q)
+
+    early = [
+        lambda: gram(0, 0), lambda: other_core(0), lambda: gram(0, 1),
+        lambda: gram(0, 2), lambda: other_core(1), lambda: other_core(2),
+    ]
+    for s in range(nz):
+        share = -(-len(early) // (nz - s))
+        for step in early[:share]:
+            step()
+        early = early[share:]
+        both(s, finish)
+    gram(0, 3)
+    other_core(3)
 
     scale = 1.0 / total
     mean_diag = jnp.sum(square[...]) * (scale / width)
@@ -319,7 +339,7 @@
     width = chans * 27
     patches = (planes // 4) * (rows_y // 4) * (cols_z // 4)
     cells = volume[0].transpose(1, 2, 0, 3)
-    weight = conv_weight.transpose(2, 0, 3, 4, 1).reshape(3 * chans, 9 * chans)
+    weight = conv_weight.transpose(2, 3, 4, 0, 1).reshape(27, chans, chans)
     padded = -(-width // 128) * 128
     space = lax.axis_size("space")
     nz = space // 4
@@ -339,6 +359,7 @@
         out_specs=pl.BlockSpec(memory_space=pltpu.VMEM),
         scratch_shapes=[
             pltpu.VMEM((rows_y, chans, cols_z), jnp.bfloat16),
+            pltpu.VMEM((3 * chans, 9 * chans), jnp.bfloat16),
             pltpu.VMEM((rows_y + 1, 3, chans, cols_z), jnp.bfloat16),
             pltpu.VMEM((planes + 1, 3 * rows_y // 4, 3 * chans, cols_z), jnp.float32),
             pltpu.VMEM((9 * chans, cols_z), jnp.bfloat16),
@@ -353,9 +374,9 @@
             dma((nz,)), dma((nz,)), dma((nz,)), dma((nz,)), dma((nz,)), dma((4, nz)),
         ],
         compiler_params=pltpu.CompilerParams(
-            collective_id=0, has_side_effects=True, vmem_limit_bytes=48 << 20
+            collective_id=0, has_side_effects=True, vmem_limit_bytes=61 << 20
         ),
-    )(cells, weight, conv_bias[:, None], basis, damping)
+    )(cells, weight, conv_bias[None, :], basis, damping)
 
 
 def body(volume, conv_weight, conv_bias, basis, damping):

time: 40.7 us -> 39.9 us (0.980); the launches traced: 40.5 us -> 39.2 us
  local copies, waits for them, and re-layouts: 6.08 us -> 4.39 us
  Pallas kernels: 33.7 us -> 34.2 us
    transpose x1 -> x0, local copies, waits for them, and re-layouts: 1.09 us -> none  [body_gather(): weight = conv_weight.transpose(2, 0, 3, 4, 1).reshape(3 * chans, 9 * chans)]
    broadcast_in_dim x1 -> x0, local copies, waits for them, and re-layouts: 0.74 us -> none  [body_gather(): conv_bias[:, None]]
    pallas_call x1, Pallas kernels: 33.7 us -> 34.2 us  [body_gather(): pl.pallas_call(functools.partial(gather_kernel, nz, total), out_shape=jax...]
    unnamed x4 -> x2, local copies, waits for them, and re-layouts: 4.06 us -> 4.39 us
where the time goes in v3:
time: 39.9 us; the launch traced here: 39.2 us
  Pallas kernels  34.2 us (86%)
  local copies, waits for them, and re-layouts  4.39 us (11%)
  between operations  0.66 us (2%)
    pallas_call x1, Pallas kernels, body_gather(): pl.pallas_call(functools.partial(gather_kernel, nz, total), out_shape=jax...  34.2 us
    unnamed x2, local copies, waits for them, and re-layouts  4.39 us

profile of v3, /device:TPU:0, one launch (start us, length us, event | category | flops | bytes accessed | tf_op | source)
XLA Modules:
  0.0 39.2 jit_solution(17673717120383070196)
XLA Ops:
  0.7 1.8 %copy.8 = bf16[1,32,4,8,128]{4,1,3,2,0:T(8,128)(2,1)} copy(bf16[1,32,4,8,128]{4,3,2,1,0:T(8,128)(2,1)} %param.5) | data formatting | bytes 524288 | tf_op args[0]
  2.4 34.2 %shard_map.55 = f32[432,864]{1,0:T(8,128)} custom-call(bf16[4,8,32,128]{3,2,1,0:T(8,128)(2,1)} %bitcast.9, bf16[27,32,32]{2,1,0:T(8,128)(2,1)} %bitcast.10, f32[1,32]{1,0:T(1,128)} %bitcast.11, f32[864,864]{1,0:T(8,128)} %basis_hbm.1, f32[1]{0:T(128)S(6)} %copy.10.damping_ref), custom_call_target="tpu_custom_call" | custom-call | tf_op jit(solution)/shard_map/pallas_call | solution.py:349
  36.6 2.6 %copy.11 = f32[432,864]{1,0:T(8,128)} copy(f32[432,864]{1,0:T(8,128)} %shard_map.55) | data formatting | bytes 2985984

commit v4 on v3

--- a/solution.py
+++ b/solution.py
@@ -374,7 +374,7 @@
             dma((nz,)), dma((nz,)), dma((nz,)), dma((nz,)), dma((nz,)), dma((4, nz)),
         ],
         compiler_params=pltpu.CompilerParams(
-            collective_id=0, has_side_effects=True, vmem_limit_bytes=61 << 20
+            collective_id=0, has_side_effects=True, vmem_limit_bytes=51 << 20
         ),
     )(cells, weight, conv_bias[None, :], basis, damping)
 

time: 39.9 us -> 37.1 us (0.930)
  Pallas kernels: 34.2 us -> 31.9 us
  local copies, waits for them, and re-layouts: 4.39 us -> 3.78 us
    pallas_call x1, Pallas kernels: 34.2 us -> 31.9 us  [body_gather(): pl.pallas_call(functools.partial(gather_kernel, nz, total), out_shape=jax...]
    unnamed x2 -> x6, local copies, waits for them, and re-layouts: 4.39 us -> 3.78 us
where the time goes in v4:
time: 37.1 us; the launch traced here: 36.4 us
  Pallas kernels  31.9 us (86%)
  local copies, waits for them, and re-layouts  3.78 us (10%)
  between operations  0.67 us (2%)
    pallas_call x1, Pallas kernels, body_gather(): pl.pallas_call(functools.partial(gather_kernel, nz, total), out_shape=jax...  31.9 us
    unnamed x6, local copies, waits for them, and re-layouts  3.78 us

profile of v4, /device:TPU:0, one launch (start us, length us, event | category | flops | bytes accessed | tf_op | source)
XLA Modules:
  0.0 36.4 jit_solution(8269044894636477202)
XLA Ops:
  0.7 1.1 %copy.8 = bf16[1,32,4,8,128]{4,1,3,2,0:T(8,128)(2,1)S(1)} copy(bf16[1,32,4,8,128]{4,3,2,1,0:T(8,128)(2,1)} %param.5) | data formatting | bytes 524288 | tf_op args[0]
  1.7 0.0 copy-start
  1.7 0.9 %copy-done = bf16[32,32,3,3,3]{1,0,4,3,2:T(8,128)(2,1)S(1)} copy-done((bf16[32,32,3,3,3]{1,0,4,3,2:T(8,128)(2,1)S(1)}, bf16[32,32,3,3,3]{1,0,4,3,2:T(8,128)(2,1)}, u32[]{:S(2)}) %copy-start) | copy-done | bytes 55320
  2.6 0.0 copy-start.1
  2.6 0.7 %copy-done.1 = f32[32]{0:T(128)S(1)} copy-done((f32[32]{0:T(128)S(1)}, f32[32]{0:T(128)}, u32[]{:S(2)}) %copy-start.1) | copy-done | bytes 152
  3.3 31.9 %shard_map.55 = f32[432,864]{1,0:T(8,128)S(1)} custom-call(bf16[4,8,32,128]{3,2,1,0:T(8,128)(2,1)S(1)} %bitcast.9, bf16[27,32,32]{2,1,0:T(8,128)(2,1)S(1)} %bitcast.10, f32[1,32]{1,0:T(1,128)S(1)} %bitcast.11, f32[864,864]{1,0:T(8,128)} %basis_hbm.1, f32[1]{0:T(128)S(6)} %copy.10.damping_ref), custom_call_target="tpu_custom_call" | custom-call | tf_op jit(solution)/shard_map/pallas_call | solution.py:349
  35.2 1.1 %copy.11 = f32[432,864]{1,0:T(8,128)} copy(f32[432,864]{1,0:T(8,128)S(1)} %shard_map.55) | data formatting | bytes 2985984
Async XLA Ops:
  1.7 0.9 %copy-start = (bf16[32,32,3,3,3]{1,0,4,3,2:T(8,128)(2,1)S(1)}, bf16[32,32,3,3,3]{1,0,4,3,2:T(8,128)(2,1)}, u32[]{:S(2)}) copy-start(bf16[32,32,3,3,3]{1,0,4,3,2:T(8,128)(2,1)} %param.6) | copy-start | bytes 165892
  2.6 0.7 %copy-start.1 = (f32[32]{0:T(128)S(1)}, f32[32]{0:T(128)}, u32[]{:S(2)}) copy-start(f32[32]{0:T(128)} %param.7) | copy-start | bytes 388

commit v5 on v4

--- a/solution.py
+++ b/solution.py
@@ -144,8 +144,8 @@
 def gather_kernel(
     nz, total, cells_ref, weight_ref, bias_ref, basis_hbm, damping_ref, out_ref,
     halo, weights, taps, partial, active, buf, acc, square, basis_f32, basis_hi, basis_lo,
-    basis_sem, halo_send, halo_recv, z_send, x_send, y_send, a_send, b_send, c_send,
-    z_recv, x_recv, y_recv, a_recv, b_recv, c_recv,
+    basis_sem, halo_send, halo_recv, z_send, x_send, y_send, a_send, b_send, c_send, d_send,
+    z_recv, x_recv, y_recv, a_recv, b_recv, c_recv, d_recv,
 ):
     vol = lax.axis_index("vol")
     space = lax.axis_index("space")
@@ -223,6 +223,9 @@
             buf.at[0, 2, k, rows], buf.at[0, 3, k, rows], b_send.at[k], b_recv.at[k], x_peer
         )
 
+    def d_copy(k, peer, way):
+        return remote(buf.at[0, 3, k], buf.at[0, 3, k], d_send.at[way, k], d_recv.at[k], peer)
+
     def c_copy(q, k):
         return remote(
             buf.at[0, q, k], buf.at[1, q, k], c_send.at[q, k], c_recv.at[q, k], core_peer
@@ -233,25 +236,33 @@
         y_copy(k).start()
         c_copy(0, k).start()
 
-    def relay(k):
+    def relay(k, s):
         x_copy(k).wait_recv()
-        a_copy(k).start()
+        if s <= 1:
+            a_copy(k).start()
         c_copy(1, k).start()
         y_copy(k).wait_recv()
-        b_copy(k).start()
+        if s <= 1:
+            b_copy(k).start()
         c_copy(2, k).start()
 
-    def finish(k):
-        a_copy(k).wait_recv()
-        b_copy(k).wait_recv()
+    def finish(k, s):
+        if s <= 1:
+            a_copy(k).wait_recv()
+            b_copy(k).wait_recv()
+        else:
+            d_copy(k, up_peer, 0).wait_recv()
+        if s >= 1:
+            pl.when((k < z) & (z + 1 < nz))(lambda: d_copy(k, up_peer, 0).start())
+            pl.when((k > z) & (z > 0))(lambda: d_copy(k, down_peer, 1).start())
         c_copy(3, k).start()
 
     def both(s, action):
         if s == 0:
-            action(z)
+            action(z, s)
             return
-        pl.when(z >= s)(lambda: action(z - s))
-        pl.when(z + s < nz)(lambda: action(z + s))
+        pl.when(z >= s)(lambda: action(z - s, s))
+        pl.when(z + s < nz)(lambda: action(z + s, s))
 
     def gram(c, q):
         block = buf[c, q].reshape(nz * patches, padded)
@@ -328,8 +339,13 @@
         pl.when((z > 0) & (k >= z))(lambda: z_copy(k, down_peer, 1).wait_send())
         x_copy(k).wait_send()
         y_copy(k).wait_send()
-        a_copy(k).wait_send()
-        b_copy(k).wait_send()
+        @pl.when((z - k <= 1) & (k - z <= 1))
+        def _():
+            a_copy(k).wait_send()
+            b_copy(k).wait_send()
+
+        pl.when((z + 1 < nz) & (k < z))(lambda: d_copy(k, up_peer, 0).wait_send())
+        pl.when((z > 0) & (k > z))(lambda: d_copy(k, down_peer, 1).wait_send())
         for q in range(4):
             c_copy(q, k).wait_send()
 
@@ -370,8 +386,8 @@
             pltpu.VMEM((width, width), jnp.bfloat16),
             pltpu.VMEM((width, width), jnp.bfloat16),
             dma, dma, dma,
-            dma((2, nz)), dma((nz,)), dma((nz,)), dma((nz,)), dma((nz,)), dma((4, nz)),
-            dma((nz,)), dma((nz,)), dma((nz,)), dma((nz,)), dma((nz,)), dma((4, nz)),
+            dma((2, nz)), dma((nz,)), dma((nz,)), dma((nz,)), dma((nz,)), dma((4, nz)), dma((2, nz)),
+            dma((nz,)), dma((nz,)), dma((nz,)), dma((nz,)), dma((nz,)), dma((4, nz)), dma((nz,)),
         ],
         compiler_params=pltpu.CompilerParams(
             collective_id=0, has_side_effects=True, vmem_limit_bytes=51 << 20

time: 37.1 us -> 40.8 us (1.100)
  Pallas kernels: 31.9 us -> 36 us
    pallas_call x1, Pallas kernels: 31.9 us -> 36 us  [body_gather(): pl.pallas_call(functools.partial(gather_kernel, nz, total), out_shape=jax...]
where the time goes in v5:
time: 40.8 us; the launch traced here: 40.4 us
  Pallas kernels  36 us (88%)
  local copies, waits for them, and re-layouts  3.78 us (9%)
  between operations  0.67 us (2%)
    pallas_call x1, Pallas kernels, body_gather(): pl.pallas_call(functools.partial(gather_kernel, nz, total), out_shape=jax...  36 us
    unnamed x6, local copies, waits for them, and re-layouts  3.78 us

profile of v5, /device:TPU:0, one launch (start us, length us, event | category | flops | bytes accessed | tf_op | source)
XLA Modules:
  0.0 40.4 jit_solution(6760110467194102660)
XLA Ops:
  0.7 1.1 %copy.8 = bf16[1,32,4,8,128]{4,1,3,2,0:T(8,128)(2,1)S(1)} copy(bf16[1,32,4,8,128]{4,3,2,1,0:T(8,128)(2,1)} %param.5) | data formatting | bytes 524288 | tf_op args[0]
  1.7 0.0 copy-start
  1.7 0.9 %copy-done = bf16[32,32,3,3,3]{1,0,4,3,2:T(8,128)(2,1)S(1)} copy-done((bf16[32,32,3,3,3]{1,0,4,3,2:T(8,128)(2,1)S(1)}, bf16[32,32,3,3,3]{1,0,4,3,2:T(8,128)(2,1)}, u32[]{:S(2)}) %copy-start) | copy-done | bytes 55320
  2.6 0.0 copy-start.1
  2.6 0.7 %copy-done.1 = f32[32]{0:T(128)S(1)} copy-done((f32[32]{0:T(128)S(1)}, f32[32]{0:T(128)}, u32[]{:S(2)}) %copy-start.1) | copy-done | bytes 152
  3.3 36.0 %shard_map.55 = f32[432,864]{1,0:T(8,128)S(1)} custom-call(bf16[4,8,32,128]{3,2,1,0:T(8,128)(2,1)S(1)} %bitcast.9, bf16[27,32,32]{2,1,0:T(8,128)(2,1)S(1)} %bitcast.10, f32[1,32]{1,0:T(1,128)S(1)} %bitcast.11, f32[864,864]{1,0:T(8,128)} %basis_hbm.1, f32[1]{0:T(128)S(6)} %copy.10.damping_ref), custom_call_target="tpu_custom_call" | custom-call | tf_op jit(solution)/shard_map/pallas_call | solution.py:365
  39.3 1.1 %copy.11 = f32[432,864]{1,0:T(8,128)} copy(f32[432,864]{1,0:T(8,128)S(1)} %shard_map.55) | data formatting | bytes 2985984
Async XLA Ops:
  1.7 0.9 %copy-start = (bf16[32,32,3,3,3]{1,0,4,3,2:T(8,128)(2,1)S(1)}, bf16[32,32,3,3,3]{1,0,4,3,2:T(8,128)(2,1)}, u32[]{:S(2)}) copy-start(bf16[32,32,3,3,3]{1,0,4,3,2:T(8,128)(2,1)} %param.6) | copy-start | bytes 165892
  2.6 0.7 %copy-start.1 = (f32[32]{0:T(128)S(1)}, f32[32]{0:T(128)}, u32[]{:S(2)}) copy-start(f32[32]{0:T(128)} %param.7) | copy-start | bytes 388
